TPU v7x, 128 devices: a whole 4x4x4 slice. The times are simulated.
128 devices in a mesh: seq: 16 (over z, x), exp: 8 (over y, core).
Axes of the slice: x: 4, y: 4, z: 4, core: 2. Of those that a mesh axis runs over, the one named last changes fastest.
Arguments:
- hidden_in: bfloat16 [16384, 2560], P(('seq', 'exp')), may hold values from -6 to 6
- grad_out: bfloat16 [16384, 2560], P(('seq', 'exp')), may hold values from -1.5 to 1.5
- expert_ids: int32 [16384, 6], P(('seq', 'exp')), may hold values from 0 to 127, as said below
- gate_weights: float32 [16384, 6], P(('seq', 'exp')), may hold values from 0.25 to 4
- w_gate: bfloat16 [128, 2560, 768], P(('seq', 'exp')), may hold values from -0.125 to 0.125
- w_up: bfloat16 [128, 2560, 768], P(('seq', 'exp')), may hold values from -0.125 to 0.125
- w_down: bfloat16 [128, 768, 2560], P(('seq', 'exp')), may hold values from -0.21875 to 0.21875
Outputs:
- grad_in: bfloat16 [16384, 2560], P(('seq', 'exp'))
- grad_gates: bfloat16 [16384, 6], P(('seq', 'exp'))
Inputs may be any that keep to these rules, and one draw needn't show every extreme that they name: `expert_ids`: expert e lies in group e // 8. Each row names 6 different experts: entries 2j and 2j + 1 (j = 0, 1, 2) lie in one group, and the three groups of a row differ. Among the 128 rows of one device each group is named by exactly 24 rows, no expert is named more than 9 times, and in every device one expert is named exactly 9 times.
All inputs are finite; a program needn't handle non-finite values.
Results may differ from a plain program's by a relative error of at most 0.0057.
Values may be sent and summed in bfloat16 or wider, within the bound.
No kernel may reach another device: no remote copies, remote signals or barrier semaphores. Data moves between devices by JAX's collectives and lax.ppermute only.
A program may use at most 128 MiB of HBM per device.

v0:
```python
import jax
import jax.numpy as jnp
from jax import lax
from jax.sharding import PartitionSpec as P


def slot_numbers(chosen, experts):
    onehot = (chosen[:, None] == jnp.arange(experts, dtype=jnp.int32)[None, :]).astype(jnp.int32)
    earlier = jnp.cumsum(onehot, axis=0) - onehot
    return jnp.sum(earlier * onehot, axis=1)


def expert_backward(rows_in, rows_grad, gate_mat, up_mat, down_mat):
    pre_gate = jnp.dot(rows_in, gate_mat, preferred_element_type=jnp.float32)
    pre_up = jnp.dot(rows_in, up_mat, preferred_element_type=jnp.float32)
    sigmoid = jax.nn.sigmoid(pre_gate)
    active = pre_gate * sigmoid
    hidden = (active * pre_up).astype(jnp.bfloat16)
    output = jnp.dot(hidden, down_mat, preferred_element_type=jnp.float32)
    gate_dot = jnp.sum(output * rows_grad.astype(jnp.float32), axis=-1).astype(jnp.bfloat16)
    contract = (((1,), (1,)), ((), ()))
    grad_hidden = lax.dot_general(rows_grad, down_mat, contract, preferred_element_type=jnp.float32)
    grad_gate = (grad_hidden * pre_up * sigmoid * (1.0 + pre_gate * (1.0 - sigmoid))).astype(
        jnp.bfloat16
    )
    grad_up = (grad_hidden * active).astype(jnp.bfloat16)
    returned = lax.dot_general(grad_gate, gate_mat, contract, preferred_element_type=jnp.float32)
    returned = returned + lax.dot_general(
        grad_up, up_mat, contract, preferred_element_type=jnp.float32
    )
    return (returned.astype(jnp.bfloat16), gate_dot)


def per_device(hidden_in, grad_out, expert_ids, gate_weights, w_gate, w_up, w_down):
    tok_rows, features = hidden_in.shape
    per_token = expert_ids.shape[1]
    experts = lax.axis_size(("seq", "exp"))
    capacity = 3 * per_token * tok_rows // (2 * experts)
    gate_mat = w_gate[0]
    up_mat = w_up[0]
    down_mat = w_down[0]
    chosen = expert_ids.reshape(-1)
    positions = chosen * capacity + slot_numbers(chosen, experts)
    send_in = (
        jnp.zeros((experts * capacity, features), jnp.bfloat16)
        .at[positions]
        .set(jnp.repeat(hidden_in, per_token, axis=0))
    )
    send_grad = (
        jnp.zeros((experts * capacity, features), jnp.bfloat16)
        .at[positions]
        .set(jnp.repeat(grad_out, per_token, axis=0))
    )
    outgoing_in = send_in.reshape(experts, capacity, features)
    outgoing_grad = send_grad.reshape(experts, capacity, features)
    rows_in = lax.all_to_all(outgoing_in, ("seq", "exp"), split_axis=0, concat_axis=0, tiled=True)
    rows_grad = lax.all_to_all(
        outgoing_grad, ("seq", "exp"), split_axis=0, concat_axis=0, tiled=True
    )
    leading = rows_in.shape[:-1]
    returned, gate_dot = expert_backward(
        rows_in.reshape(-1, features), rows_grad.reshape(-1, features), gate_mat, up_mat, down_mat
    )
    returned, gate_dot = (returned.reshape(leading + (features,)), gate_dot.reshape(leading))
    returned, gate_dot = (
        lax.all_to_all(returned, ("seq", "exp"), split_axis=0, concat_axis=0, tiled=True),
        lax.all_to_all(gate_dot, ("seq", "exp"), split_axis=0, concat_axis=0, tiled=True),
    )
    picked = returned.reshape(experts * capacity, features)[positions]
    weighted = (
        picked.astype(jnp.float32).reshape(tok_rows, per_token, features) * gate_weights[:, :, None]
    )
    grad_in = jnp.sum(weighted, axis=1).astype(jnp.bfloat16)
    grad_gates = gate_dot.reshape(-1)[positions].reshape(tok_rows, per_token)
    return (grad_in, grad_gates)


def solution(mesh):
    in_specs = (
        P(("seq", "exp"), None),
        P(("seq", "exp"), None),
        P(("seq", "exp"), None),
        P(("seq", "exp"), None),
        P(("seq", "exp"), None, None),
        P(("seq", "exp"), None, None),
        P(("seq", "exp"), None, None),
    )
    out_specs = (P(("seq", "exp"), None), P(("seq", "exp"), None))
    return jax.shard_map(
        per_device, mesh=mesh, in_specs=in_specs, out_specs=out_specs, check_vma=False
    )
```

profile of v0, /device:TPU:1, one launch (start us, length us, event | category | flops | bytes accessed | tf_op | source)
XLA Modules:
  0.0 555.5 jit_solution(15400630997214130017)
XLA Ops:
  0.6 0.7 broadcast_multiply_fusion
  1.3 0.8 copy.18
  2.1 0.1 eq.29
  2.3 0.1 eq.25
  2.4 0.1 copy.17
  2.5 0.1 mul.53
  2.6 0.1 copy.20
  2.8 0.2 fusion.22
  3.0 0.1 copy.21
  3.1 4.0 broadcast_in_dim.5
  7.1 7.2 %reshape.141 = bf16[768,2560]{1,0:T(8,128)(2,1)} reshape(bf16[128,6,2560]{2,1,0:T(8,128)(2,1)} %broadcast_in_dim.5) | data formatting | bytes 7864320 | tf_op jit(solution)/shard_map/reshape | solution.py:47
  14.4 0.3 fusion.25
  14.7 12.7 %scatter_custom_fusion.1 = bf16[1152,2560]{1,0:T(8,128)(2,1)} fusion(s32[768]{0:T(1024)S(1)} %fusion.27, bf16[768,2560]{1,0:T(8,128)(2,1)} %reshape.141, bf16[]{:T(256)} %constant.6.clone.1), kind=kCustom, calls=%fused_computation.23 | custom fusion | bytes 5898752 | tf_op jit(solution)/shard_map/scatter | solution.py:47
  27.4 9.0 %reshape.106 = bf16[128,9,2560]{2,1,0:T(8,128)(2,1)} reshape(bf16[1152,2560]{1,0:T(8,128)(2,1)} %scatter_custom_fusion.1) | data formatting | bytes 11796480 | tf_op jit(solution)/shard_map/reshape | solution.py:54
  36.4 0.0 copy-start.2
  36.4 12.2 %all-to-all-start.1 = ((bf16[128,9,2560]{2,1,0:T(8,128)(2,1)}), bf16[128,9,2560]{2,1,0:T(8,128)(2,1)}, u32[]{:S(2)}, u32[]{:S(2)}) async-start(bf16[128,9,2560]{2,1,0:T(8,128)(2,1)} %reshape.106), calls=%async_computation.1 | async-start | bytes 20971520 | tf_op jit(solution)/shard_map/all_to_all | solution.py:56
  48.6 0.0 copy-done.2
  48.7 3.0 broadcast_in_dim.4
  51.6 7.2 %reshape.133 = bf16[768,2560]{1,0:T(8,128)(2,1)} reshape(bf16[128,6,2560]{2,1,0:T(8,128)(2,1)} %broadcast_in_dim.4) | data formatting | bytes 7864320 | tf_op jit(solution)/shard_map/reshape | solution.py:52
  58.8 12.7 %scatter_custom_fusion = bf16[1152,2560]{1,0:T(8,128)(2,1)} fusion(s32[768]{0:T(1024)S(1)} %fusion.27, bf16[768,2560]{1,0:T(8,128)(2,1)} %reshape.133, bf16[]{:T(256)} %constant.6.clone.1), kind=kCustom, calls=%fused_computation.25 | custom fusion | bytes 5898752 | tf_op jit(solution)/shard_map/scatter | solution.py:52
  71.6 9.0 %reshape.103 = bf16[128,9,2560]{2,1,0:T(8,128)(2,1)} reshape(bf16[1152,2560]{1,0:T(8,128)(2,1)} %scatter_custom_fusion) | data formatting | bytes 11796480 | tf_op jit(solution)/shard_map/reshape | solution.py:55
  80.6 93.5 %all-to-all-done.1 = bf16[128,9,2560]{2,1,0:T(8,128)(2,1)} async-done(((bf16[128,9,2560]{2,1,0:T(8,128)(2,1)}), bf16[128,9,2560]{2,1,0:T(8,128)(2,1)}, u32[]{:S(2)}, u32[]{:S(2)}) %all-to-all-start.1) | async-done | bytes 5898272 | tf_op jit(solution)/shard_map/all_to_all | solution.py:56
  174.0 7.9 %all-to-all-start = ((bf16[128,9,2560]{2,1,0:T(8,128)(2,1)}), bf16[128,9,2560]{2,1,0:T(8,128)(2,1)}, u32[]{:S(2)}, u32[]{:S(2)}) async-start(bf16[128,9,2560]{2,1,0:T(8,128)(2,1)} %reshape.103), calls=%async_computation | async-start | bytes 20971520 | tf_op jit(solution)/shard_map/all_to_all | solution.py:57
  181.9 9.5 %reshape.107 = bf16[1152,2560]{1,0:T(8,128)(2,1)} reshape(bf16[128,9,2560]{2,1,0:T(8,128)(2,1)} %all-to-all-done.1) | data formatting | bytes 11796480 | tf_op jit(solution)/shard_map/reshape | solution.py:62
  191.5 0.0 copy-start
  191.5 0.0 copy-start.5
  191.5 10.5 %fusion.3 = f32[1152,768]{1,0:T(8,128)} fusion(bf16[1152,2560]{1,0:T(8,128)(2,1)} %reshape.107, bf16[1,2560,768]{2,1,0:T(8,128)(2,1)} %param.11), kind=kOutput, calls=%fused_computation.10 | convolution fusion | flops 4529848320 | bytes 13369344 | tf_op jit(solution)/shard_map/dot_general | solution.py:14
  202.0 0.0 copy-done
  202.0 0.0 copy-done.5
  202.0 6.6 %fusion.6 = f32[1152,768]{1,0:T(8,128)} fusion(bf16[1152,2560]{1,0:T(8,128)(2,1)S(1)} %copy-done, bf16[1,2560,768]{2,1,0:T(8,128)(2,1)S(1)} %copy-done.5), kind=kOutput, calls=%fused_computation.13 | convolution fusion | flops 4529848320 | bytes 13369344 | tf_op jit(solution)/shard_map/dot_general | solution.py:15
  208.6 98.7 %all-to-all-done = bf16[128,9,2560]{2,1,0:T(8,128)(2,1)} async-done(((bf16[128,9,2560]{2,1,0:T(8,128)(2,1)}), bf16[128,9,2560]{2,1,0:T(8,128)(2,1)}, u32[]{:S(2)}, u32[]{:S(2)}) %all-to-all-start) | async-done | bytes 5898272 | tf_op jit(solution)/shard_map/all_to_all | solution.py:57
  307.3 9.5 %reshape.104 = bf16[1152,2560]{1,0:T(8,128)(2,1)} reshape(bf16[128,9,2560]{2,1,0:T(8,128)(2,1)} %all-to-all-done) | data formatting | bytes 11796480 | tf_op jit(solution)/shard_map/reshape | solution.py:62
  316.8 0.0 copy-start.1
  316.8 0.0 copy-start.4
  316.8 0.0 copy-start.6
  316.8 0.0 copy-start.7
  316.8 10.6 %fusion.9 = f32[1152,768]{1,0:T(8,128)} fusion(bf16[1152,2560]{1,0:T(8,128)(2,1)} %reshape.104, bf16[1,768,2560]{2,1,0:T(8,128)(2,1)} %param.13), kind=kOutput, calls=%fused_computation.16 | convolution fusion | flops 4529848320 | bytes 13369344 | tf_op jit(solution)/shard_map/dot_general | solution.py:22
  327.4 0.0 copy-done.1
  327.4 0.0 copy-done.4
  327.4 0.0 copy-done.6
  327.4 0.0 copy-done.7
  327.4 6.7 %fusion.16 = bf16[1152]{0:T(1024)(128)(2,1)S(1)} fusion(bf16[1152,2560]{1,0:T(8,128)(2,1)S(1)} %copy-done.1, bf16[1,768,2560]{2,1,0:T(8,128)(2,1)S(1)} %copy-done.4, f32[1152,768]{1,0:T(8,128)S(1)} %copy-done.7, f32[1152,768]{1,0:T(8,128)S(1)} %copy-done.6), kind=kOutput, calls=%fused_computation.27 | convolution fusion | flops 4544003072 | bytes 16910592 | tf_op jit(solution)/shard_map/dot_general | solution.py:19
  334.2 0.9 convert_element_type.59
  335.1 7.1 %all-to-all-start.3 = ((bf16[128,1,9]{2,1,0:T(2,128)(2,1)}), bf16[128,1,9]{2,1,0:T(2,128)(2,1)S(1)}, u32[]{:S(2)}, u32[]{:S(2)}) async-start(bf16[128,1,9]{2,1,0:T(2,128)(2,1)} %convert_element_type.59), calls=%async_computation.3 | async-start | bytes 131072 | tf_op jit(solution)/shard_map/all_to_all | solution.py:67
  342.2 15.3 %fusion.1 = f32[1152,2560]{1,0:T(8,128)} fusion(bf16[1,2560,768]{2,1,0:T(8,128)(2,1)} %param.11, f32[1152,768]{1,0:T(8,128)} %fusion.3, f32[1152,768]{1,0:T(8,128)} %fusion.9, f32[1152,768]{1,0:T(8,128)} %fusion.6), kind=kOutput, calls=%fused_computation.8 | convolution fusion | flops 4538695680 | bytes 26345472 | tf_op jit(solution)/shard_map/dot_general | solution.py:27
  357.4 15.0 %fusion = bf16[1152,2560]{1,0:T(8,128)(2,1)} fusion(f32[1152,2560]{1,0:T(8,128)} %fusion.1, bf16[1,2560,768]{2,1,0:T(8,128)(2,1)} %param.12, f32[1152,768]{1,0:T(8,128)} %fusion.9, f32[1152,768]{1,0:T(8,128)} %fusion.3), kind=kOutput, calls=%fused_computation.6 | convolution fusion | flops 4541054976 | bytes 28704768 | tf_op jit(solution)/shard_map/dot_general | solution.py:28
  372.5 9.0 %reshape.108 = bf16[128,9,2560]{2,1,0:T(8,128)(2,1)} reshape(bf16[1152,2560]{1,0:T(8,128)(2,1)} %fusion) | data formatting | bytes 11796480 | tf_op jit(solution)/shard_map/reshape | solution.py:64
  381.5 0.0 copy-start.3
  381.5 0.0 all-to-all-done.3
  381.5 10.5 %all-to-all-start.2 = ((bf16[128,9,2560]{2,1,0:T(8,128)(2,1)}), bf16[128,9,2560]{2,1,0:T(8,128)(2,1)}, u32[]{:S(2)}, u32[]{:S(2)}) async-start(bf16[128,9,2560]{2,1,0:T(8,128)(2,1)} %reshape.108), calls=%async_computation.2 | async-start | bytes 20971520 | tf_op jit(solution)/shard_map/all_to_all | solution.py:66
  392.0 0.0 copy-done.3
  392.0 0.1 copy.22
  392.1 0.2 reduce.1
  392.3 0.2 reshape.110
  392.5 5.0 gather_fusion.1
  397.5 0.1 reshape.111
  397.7 0.7 copy.24
  398.3 119.0 %all-to-all-done.2 = bf16[128,9,2560]{2,1,0:T(8,128)(2,1)} async-done(((bf16[128,9,2560]{2,1,0:T(8,128)(2,1)}), bf16[128,9,2560]{2,1,0:T(8,128)(2,1)}, u32[]{:S(2)}, u32[]{:S(2)}) %all-to-all-start.2) | async-done | bytes 5898272 | tf_op jit(solution)/shard_map/all_to_all | solution.py:66
  517.4 9.5 %reshape.109 = bf16[1152,2560]{1,0:T(8,128)(2,1)} reshape(bf16[128,9,2560]{2,1,0:T(8,128)(2,1)} %all-to-all-done.2) | data formatting | bytes 11796480 | tf_op jit(solution)/shard_map/reshape | solution.py:69
  526.9 11.8 %gather_fusion = bf16[768,2560]{1,0:T(8,128)(2,1)} fusion(bf16[1152,2560]{1,0:T(8,128)(2,1)} %reshape.109, s32[1024]{0:T(1024)S(1)} %pad_clamp_fusion), kind=kCustom, calls=%fused_computation | custom fusion | bytes 7867392 | tf_op jit(solution)/shard_map/gather | solution.py:69
  538.7 7.8 %reshape.112 = f32[128,6,2560]{2,1,0:T(8,128)} reshape(bf16[768,2560]{1,0:T(8,128)(2,1)} %gather_fusion) | data formatting | bytes 11796480 | tf_op jit(solution)/shard_map/convert_element_type | solution.py:71
  546.5 8.8 %multiply_reduce_fusion = bf16[128,2560]{1,0:T(8,128)(2,1)} fusion(f32[128,6,2560]{2,1,0:T(8,128)} %reshape.112, f32[128,6]{1,0:T(8,128)S(1)} %copy.22), kind=kLoop, calls=%fused_computation.7 | loop fusion | flops 3604480 | bytes 8522752 | tf_op jit(solution)/shard_map/reduce_sum | solution.py:73
  (5 shorter events, 0.1 us)
Async XLA Ops:
  36.4 12.3 %copy-start.2 = (bf16[128,2560]{1,0:T(8,128)(2,1)S(1)}, bf16[128,2560]{1,0:T(8,128)(2,1)}, u32[]{:S(2)}) copy-start(bf16[128,2560]{1,0:T(8,128)(2,1)} %param.8) | copy-start | bytes 1966084
  36.4 137.6 %all-to-all-start.1 = ((bf16[128,9,2560]{2,1,0:T(8,128)(2,1)}), bf16[128,9,2560]{2,1,0:T(8,128)(2,1)}, u32[]{:S(2)}, u32[]{:S(2)}) async-start(bf16[128,9,2560]{2,1,0:T(8,128)(2,1)} %reshape.106), calls=%async_computation.1 | async-start | bytes 20971520 | tf_op jit(solution)/shard_map/all_to_all | solution.py:56
  174.0 133.3 %all-to-all-start = ((bf16[128,9,2560]{2,1,0:T(8,128)(2,1)}), bf16[128,9,2560]{2,1,0:T(8,128)(2,1)}, u32[]{:S(2)}, u32[]{:S(2)}) async-start(bf16[128,9,2560]{2,1,0:T(8,128)(2,1)} %reshape.103), calls=%async_computation | async-start | bytes 20971520 | tf_op jit(solution)/shard_map/all_to_all | solution.py:57
  191.5 10.5 %copy-start = (bf16[1152,2560]{1,0:T(8,128)(2,1)S(1)}, bf16[1152,2560]{1,0:T(8,128)(2,1)}, u32[]{:S(2)}) copy-start(bf16[1152,2560]{1,0:T(8,128)(2,1)} %reshape.107) | copy-start | bytes 17694724
  191.5 10.5 %copy-start.5 = (bf16[1,2560,768]{2,1,0:T(8,128)(2,1)S(1)}, bf16[1,2560,768]{2,1,0:T(8,128)(2,1)}, u32[]{:S(2)}) copy-start(bf16[1,2560,768]{2,1,0:T(8,128)(2,1)} %param.12) | copy-start | bytes 11796484
  316.8 10.6 %copy-start.1 = (bf16[1152,2560]{1,0:T(8,128)(2,1)S(1)}, bf16[1152,2560]{1,0:T(8,128)(2,1)}, u32[]{:S(2)}) copy-start(bf16[1152,2560]{1,0:T(8,128)(2,1)} %reshape.104) | copy-start | bytes 17694724
  316.8 10.6 %copy-start.4 = (bf16[1,768,2560]{2,1,0:T(8,128)(2,1)S(1)}, bf16[1,768,2560]{2,1,0:T(8,128)(2,1)}, u32[]{:S(2)}) copy-start(bf16[1,768,2560]{2,1,0:T(8,128)(2,1)} %param.13) | copy-start | bytes 11796484
  316.8 10.6 %copy-start.6 = (f32[1152,768]{1,0:T(8,128)S(1)}, f32[1152,768]{1,0:T(8,128)}, u32[]{:S(2)}) copy-start(f32[1152,768]{1,0:T(8,128)} %fusion.3) | copy-start | bytes 10616836
  316.8 10.6 %copy-start.7 = (f32[1152,768]{1,0:T(8,128)S(1)}, f32[1152,768]{1,0:T(8,128)}, u32[]{:S(2)}) copy-start(f32[1152,768]{1,0:T(8,128)} %fusion.6) | copy-start | bytes 10616836
  335.1 46.4 %all-to-all-start.3 = ((bf16[128,1,9]{2,1,0:T(2,128)(2,1)}), bf16[128,1,9]{2,1,0:T(2,128)(2,1)S(1)}, u32[]{:S(2)}, u32[]{:S(2)}) async-start(bf16[128,1,9]{2,1,0:T(2,128)(2,1)} %convert_element_type.59), calls=%async_computation.3 | async-start | bytes 131072 | tf_op jit(solution)/shard_map/all_to_all | solution.py:67
  381.5 10.5 %copy-start.3 = (f32[128,6]{0,1:T(8,128)S(1)}, f32[128,6]{0,1:T(8,128)}, u32[]{:S(2)}) copy-start(f32[128,6]{0,1:T(8,128)} %param.10) | copy-start | bytes 9220
  381.5 135.9 %all-to-all-start.2 = ((bf16[128,9,2560]{2,1,0:T(8,128)(2,1)}), bf16[128,9,2560]{2,1,0:T(8,128)(2,1)}, u32[]{:S(2)}, u32[]{:S(2)}) async-start(bf16[128,9,2560]{2,1,0:T(8,128)(2,1)} %reshape.108), calls=%async_computation.2 | async-start | bytes 20971520 | tf_op jit(solution)/shard_map/all_to_all | solution.py:66
where the time goes:
time: 566 us; the launch traced here: 556 us
  waiting for transfers between devices  311 us (55%)
  local copies, waits for them, and re-layouts  131 us (23%)
  matrix products  64.7 us (11%)
  starting transfers between devices  37.7 us (7%)
  other arithmetic  10.3 us (2%)
    all_to_all x1, waiting for transfers between devices, per_device(): lax.all_to_all(returned, ('seq', 'exp'), split_axis=0, concat_axis=0, til...  119 us
    all_to_all x1, waiting for transfers between devices, per_device(): lax.all_to_all(outgoing_grad, ('seq', 'exp'), split_axis=0, concat_axis=0...  98.7 us
    all_to_all x1, waiting for transfers between devices, per_device(): lax.all_to_all(outgoing_in, ('seq', 'exp'), split_axis=0, concat_axis=0,...  93.5 us
    dot_general x1, matrix products, expert_backward(): lax.dot_general(grad_gate, gate_mat, contract, preferred_element_type=jnp...  15.3 us
    dot_general x1, matrix products, expert_backward(): lax.dot_general(grad_up, up_mat, contract, preferred_element_type=jnp.flo...  15 us
    scatter x1, local copies, waits for them, and re-layouts, per_device(): send_grad = jnp.zeros((experts * capacity, features), jnp.bfloat16).at[po...  12.7 us
    scatter x1, local copies, waits for them, and re-layouts, per_device(): send_in = jnp.zeros((experts * capacity, features), jnp.bfloat16).at[posi...  12.7 us
    all_to_all x1, starting transfers between devices, per_device(): lax.all_to_all(outgoing_in, ('seq', 'exp'), split_axis=0, concat_axis=0,...  12.2 us
  transfers between devices with their start and end apart: 4, of which 3 were waited for; matrix products, arithmetic and copies ran while one was open for 19% of the time, Pallas kernels for 0%

commit v1 on v0

v1 whole, which is shorter than its diff:
```python
import jax
import jax.numpy as jnp
from jax import lax
from jax.sharding import PartitionSpec as P

BF = jnp.bfloat16
F32 = jnp.float32
LANES = 128


def dot(a, b):
    return jnp.dot(a, b, preferred_element_type=F32)


def dot_t(a, b):
    return lax.dot_general(a, b, (((0,), (0,)), ((), ())), preferred_element_type=F32)


def dot_nt(a, b):
    return lax.dot_general(a, b, (((1,), (1,)), ((), ())), preferred_element_type=F32)


def earlier_counts(names):
    n = names.shape[-2]
    lower = (jnp.arange(n)[:, None] > jnp.arange(n)[None, :]).astype(BF)
    counts = jnp.einsum("ij,...jm->...im", lower, names.astype(BF), preferred_element_type=F32)
    return jnp.where(names, counts, -1.0)


def weight_parts(weights):
    first = lax.reduce_precision(weights, 8, 7)
    rest = weights - first
    second = lax.reduce_precision(rest, 8, 7)
    third = lax.reduce_precision(rest - second, 8, 7)
    return first, second, third


def exchange(blocks, n_exp):
    out = [blocks[0]]
    for k in range(1, n_exp):
        out.append(lax.ppermute(blocks[k], "exp", [(i, i ^ k) for i in range(n_exp)]))
    return out


def per_device(hidden_in, grad_out, expert_ids, gate_weights, w_gate, w_up, w_down):
    n_tok, features = hidden_in.shape
    top = expert_ids.shape[1]
    n_seq, n_exp = lax.axis_size("seq"), lax.axis_size("exp")
    group, member = lax.axis_index("seq"), lax.axis_index("exp")
    experts = n_seq * n_exp
    cap = 3 * top * n_tok // (2 * experts)
    per_group = top // 2 * n_tok // n_seq
    half = features // 2
    gate_mat, up_mat, down_mat = w_gate[0], w_up[0], w_down[0]

    meta = jnp.concatenate(
        (expert_ids.astype(F32),) + weight_parts(gate_weights)
        + (jnp.zeros((n_tok, LANES - 4 * top), F32),), axis=1).astype(BF)

    def read_meta(lanes):
        lanes = lanes.astype(F32)
        ids = lanes[:, :top]
        weights = lanes[:, top:2 * top] + lanes[:, 2 * top:3 * top] + lanes[:, 3 * top:4 * top]
        return ids, weights

    column = lax.all_gather(jnp.concatenate((grad_out, meta), axis=1), "exp", axis=0, tiled=True)

    group_ids = expert_ids // n_exp
    in_group = jnp.any(group_ids[:, :, None] == jnp.arange(n_seq)[None, None, :], axis=1)
    group_rank = earlier_counts(in_group).T
    pick = (group_rank[:, None, :] == jnp.arange(per_group, dtype=F32)[None, :, None])
    pick = pick.astype(BF).reshape(n_seq * per_group, n_tok)
    send = dot(pick, jnp.concatenate((hidden_in, meta), axis=1)).astype(BF)
    hub = lax.all_to_all(send.reshape(n_seq, per_group, features + LANES), "seq", 0, 0, tiled=True)
    hub = hub.reshape(n_seq * per_group, features + LANES)

    hub_ids, hub_weights = read_meta(hub[:, features:])
    local = jnp.arange(n_exp) + group * n_exp
    hits = hub_ids[:, :, None] == local.astype(F32)[None, None, :]
    named = jnp.any(hits, axis=1)
    weight_a = jnp.sum(jnp.where(hits, hub_weights[:, :, None], 0.0), axis=1)
    rank = earlier_counts(named.reshape(n_seq, per_group, n_exp)).reshape(n_seq * per_group, n_exp)
    block = (jnp.arange(n_seq * per_group) // per_group).astype(F32)
    slot_a = jnp.where(named, block[:, None] * cap + rank, -1.0)
    rows_a = n_seq * cap
    place = jnp.arange(rows_a, dtype=F32)
    put_a, wput_a = [], []
    for k in range(n_exp):
        mine = (jnp.arange(n_exp) == (member ^ k))[None, :]
        slot_k = jnp.sum(jnp.where(mine, slot_a, 0.0), axis=1)
        weight_k = jnp.sum(jnp.where(mine, weight_a, 0.0), axis=1)
        hot = slot_k[None, :] == place[:, None]
        put_a.append(hot)
        wput_a.append(jnp.where(hot, weight_k[None, :], 0.0))
    blocks = [dot(hot.astype(BF), hub[:, :features]).astype(BF) for hot in put_a]
    rows_in = jnp.concatenate(exchange(blocks, n_exp), axis=0)

    col_ids, col_weights = read_meta(column[:, features:])
    theirs = (jnp.arange(n_seq) * n_exp + member).astype(F32)
    hits_b = col_ids[:, :, None] == theirs[None, None, :]
    named_b = jnp.any(hits_b, axis=1)
    weight_b = jnp.sum(jnp.where(hits_b, col_weights[:, :, None], 0.0), axis=1)
    rank_b = earlier_counts(named_b.reshape(n_exp, n_tok, n_seq)).reshape(n_exp * n_tok, n_seq)
    order = (jnp.arange(n_exp * n_tok) // n_tok) ^ member
    slot_b = jnp.where(named_b, order[:, None].astype(F32) * cap + rank_b, -1.0)
    rows_b = n_exp * cap
    put_b = slot_b.T[:, None, :] == jnp.arange(rows_b, dtype=F32)[None, :, None]
    send_b = dot(put_b.astype(BF).reshape(n_seq * rows_b, n_exp * n_tok), column[:, :features]).astype(BF)
    recv_b = lax.all_to_all(send_b.reshape(n_seq, rows_b, features), "seq", 0, 0, tiled=True)
    recv_b = recv_b.reshape(n_seq * rows_b, features)

    total = n_seq * n_exp * cap
    row = jnp.arange(total)
    k_of, s_of, c_of = row // rows_a, row % rows_a // cap, row % cap
    order_a = (s_of * rows_b + k_of * cap + c_of)[:, None] == row[None, :]
    order_a = order_a.astype(BF)
    rows_grad = dot(order_a, recv_b).astype(BF)

    pre_gate = dot(rows_in, gate_mat)
    pre_up = dot(rows_in, up_mat)
    sigmoid = jax.nn.sigmoid(pre_gate)
    active = pre_gate * sigmoid
    hidden = (active * pre_up).astype(BF)
    grad_hidden = dot_nt(rows_grad, down_mat)
    gate_dot = jnp.sum(hidden.astype(F32) * grad_hidden, axis=1).astype(BF)
    grad_gate = (grad_hidden * pre_up * sigmoid * (1.0 + pre_gate * (1.0 - sigmoid))).astype(BF)
    grad_up = (grad_hidden * active).astype(BF)
    returned = (dot_nt(grad_gate, gate_mat) + dot_nt(grad_up, up_mat)).astype(BF)
    lane = jnp.arange(LANES) == group * n_exp + member
    gate_lanes = jnp.where(lane[None, :], gate_dot[:, None], jnp.zeros((), BF))

    back_a = jnp.concatenate((returned[:, :half], gate_lanes), axis=1)
    got = exchange([back_a[k * rows_a:(k + 1) * rows_a] for k in range(n_exp)], n_exp)
    got = jnp.concatenate(got, axis=0)
    hot_a = jnp.concatenate(put_a, axis=0).astype(BF)
    weights_a = jnp.concatenate(wput_a, axis=0)
    first, second, _ = weight_parts(weights_a)
    sums = dot_t(first.astype(BF), got[:, :half]) + dot_t(second.astype(BF), got[:, :half])
    gates = dot_t(hot_a, got[:, half:])
    back = jnp.concatenate((sums, gates), axis=1).astype(BF)
    back = lax.all_to_all(back.reshape(n_seq, per_group, half + LANES), "seq", 0, 0, tiled=True)
    final_a = dot_t(pick, back.reshape(n_seq * per_group, half + LANES))

    back_b = dot_t(order_a, returned[:, half:]).astype(BF)
    got_b = lax.all_to_all(back_b.reshape(n_seq, rows_b, half), "seq", 0, 0, tiled=True)
    got_b = got_b.reshape(n_seq * rows_b, half)
    parts = []
    for k in range(n_exp):
        start = (member ^ k) * n_tok
        slot_k = lax.dynamic_slice_in_dim(slot_b, start, n_tok, 0)
        weight_k = lax.dynamic_slice_in_dim(weight_b, start, n_tok, 0)
        hot = slot_k[:, :, None] == jnp.arange(rows_b, dtype=F32)[None, None, :]
        mixed = jnp.where(hot, weight_k[:, :, None], 0.0).reshape(n_tok, n_seq * rows_b)
        first, second, _ = weight_parts(mixed)
        parts.append((dot(first.astype(BF), got_b) + dot(second.astype(BF), got_b)).astype(BF))
    final_b = sum(p.astype(F32) for p in exchange(parts, n_exp))

    grad_in = jnp.concatenate((final_a[:, :half], final_b), axis=1).astype(BF)
    table = final_a[:, half:]
    chosen = expert_ids[:, :, None] == jnp.arange(experts)[None, None, :]
    grad_gates = jnp.sum(jnp.where(chosen, table[:, None, :experts], 0.0), axis=2).astype(BF)
    return grad_in, grad_gates


def solution(mesh):
    rows, mats = P(("seq", "exp"), None), P(("seq", "exp"), None, None)
    return jax.shard_map(
        per_device, mesh=mesh, in_specs=(rows,) * 4 + (mats,) * 3, out_specs=(rows, rows), check_vma=False
    )
```

time: 566 us -> 447 us (0.79)
  waiting for transfers between devices: 311 us -> 192 us
  local copies, waits for them, and re-layouts: 131 us -> 26.2 us
  matrix products: 64.7 us -> 122 us
  other arithmetic: 10.3 us -> 29.1 us
  starting transfers between devices: 37.7 us -> 56.4 us
  between operations: 0.97 us -> 15 us
    all_to_all x4, waiting for transfers between devices: 311 us -> 103 us  [the longest x1 40 us: per_device(): lax.all_to_all(back_b.reshape(n_seq, rows_b, half), 'seq', 0, 0, tiled=True)]
    ppermute x0 -> x21, waiting for transfers between devices: none -> 89.5 us  [exchange(): lax.ppermute(blocks[k], 'exp', [(i, i ^ k) for i in range(n_exp)])]
    reshape x10 -> x0, local copies, waits for them, and re-layouts: 70.4 us -> none  [the longest x1 9.55 us: per_device(): picked = returned.reshape(experts * capacity, features)[positions]]
    dot_general x6 -> x39, matrix products: 64.7 us -> 122 us  [the longest x28 52.8 us: dot(): return jnp.dot(a, b, preferred_element_type=F32)]
    ppermute x0 -> x21, starting transfers between devices: none -> 35.9 us  [exchange(): lax.ppermute(blocks[k], 'exp', [(i, i ^ k) for i in range(n_exp)])]
    scatter x2 -> x0, local copies, waits for them, and re-layouts: 25.4 us -> none  [the longest x1 12.7 us: per_device(): send_grad = jnp.zeros((experts * capacity, features), jnp.bfloat16).at[po...]
    all_to_all x4, starting transfers between devices: 37.7 us -> 20.5 us  [the longest x1 8.43 us: per_device(): lax.all_to_all(send.reshape(n_seq, per_group, features + LANES), 'seq', 0...]
    gather x2 -> x0, local copies, waits for them, and re-layouts: 16.8 us -> none  [the longest x1 11.8 us: per_device(): picked = returned.reshape(experts * capacity, features)[positions]]
  transfers between devices with their start and end apart: 4 -> 26, of which waited for: 3 -> 17; matrix products, arithmetic and copies ran while one was open for 19% -> 24% of each run, Pallas kernels for 0% -> 0%
where the time goes in v1:
time: 447 us; the launch traced here: 441 us
  waiting for transfers between devices  192 us (43%)
  matrix products  122 us (27%)
  starting transfers between devices  56.4 us (13%)
  other arithmetic  29.1 us (7%)
  local copies, waits for them, and re-layouts  26.2 us (6%)
  between operations  15 us (3%)
    ppermute x21, waiting for transfers between devices, exchange(): lax.ppermute(blocks[k], 'exp', [(i, i ^ k) for i in range(n_exp)])  89.5 us
    dot_general x28, matrix products, dot(): return jnp.dot(a, b, preferred_element_type=F32)  52.8 us
    dot_general x3, matrix products, dot_nt(): lax.dot_general(a, b, (((1,), (1,)), ((), ())), preferred_element_type=F32)  51.6 us
    all_to_all x1, waiting for transfers between devices, per_device(): lax.all_to_all(back_b.reshape(n_seq, rows_b, half), 'seq', 0, 0, tiled=True)  40 us
    ppermute x21, starting transfers between devices, exchange(): lax.ppermute(blocks[k], 'exp', [(i, i ^ k) for i in range(n_exp)])  35.9 us
    all_to_all x1, waiting for transfers between devices, per_device(): lax.all_to_all(send.reshape(n_seq, per_group, features + LANES), 'seq', 0...  26.8 us
    all_to_all x1, waiting for transfers between devices, per_device(): lax.all_to_all(send_b.reshape(n_seq, rows_b, features), 'seq', 0, 0, tile...  24.9 us
    dot_general x5, matrix products, dot_t(): lax.dot_general(a, b, (((0,), (0,)), ((), ())), preferred_element_type=F32)  16.2 us
  transfers between devices with their start and end apart: 26, of which 17 were waited for; matrix products, arithmetic and copies ran while one was open for 24% of the time, Pallas kernels for 0%

profile of v1, /device:TPU:1, one launch (start us, length us, event | category | flops | bytes accessed | tf_op | source)
XLA Modules:
  0.0 440.7 jit_solution(13167520169900770799)
XLA Ops:
  9.2 2.0 concatenate.40
  13.4 2.0 convolution_convert_fusion.3
  15.4 8.4 %all-to-all-start = ((bf16[16,24,2688]{2,1,0:T(8,128)(2,1)}), bf16[16,24,2688]{2,1,0:T(8,128)(2,1)S(1)}, u32[]{:S(2)}, u32[]{:S(2)}) async-start(bf16[16,24,2688]{2,1,0:T(8,128)(2,1)} %bitcast.2), calls=%async_computation | async-start | bytes 4128768 | tf_op jit(solution)/shard_map/all_to_all | solution.py:74
  27.1 26.8 %all-to-all-done = bf16[16,24,2688]{2,1,0:T(8,128)(2,1)S(1)} async-done(((bf16[16,24,2688]{2,1,0:T(8,128)(2,1)}), bf16[16,24,2688]{2,1,0:T(8,128)(2,1)S(1)}, u32[]{:S(2)}, u32[]{:S(2)}) %all-to-all-start) | async-done | bytes 2064416 | tf_op jit(solution)/shard_map/all_to_all | solution.py:74
  56.5 1.4 convolution_convert_fusion.10
  57.9 2.1 collective-permute-start
  60.8 1.5 convolution_convert_fusion.9
  64.3 1.4 convolution_convert_fusion.8
  66.8 1.4 convolution_convert_fusion.7
  68.3 2.9 collective-permute-start.3
  71.2 1.4 eq.502
  72.6 2.1 convolution_convert_fusion.6
  75.4 1.4 eq.508
  79.1 1.4 select_reduce_fusion.9
  82.7 1.5 select_dynamic-update-slice_fusion.7
  85.5 1.4 select_dynamic-update-slice_fusion.5
  86.9 1.4 select_dynamic-update-slice_fusion.4
  88.3 1.4 select_dynamic-update-slice_fusion.3
  89.7 1.4 select_dynamic-update-slice_fusion.2
  91.1 1.4 select_dynamic-update-slice_fusion.1
  92.5 2.1 fusion.11
  94.6 1.4 convolution_convert_fusion.5
  96.0 1.4 convolution_convert_fusion.4
  100.2 10.5 %convolution_convert_fusion.1 = bf16[1152,2560]{1,0:T(8,128)(2,1)} fusion(pred[1152,1024]{1,0:T(32,128)(4,1)S(1)} %bitcast_compare_fusion, bf16[1024,2688]{1,0:T(8,128)(2,1)} %all-gather.2.cloned.1.call-done), kind=kOutput, calls=%fused_computation.3 | convolution fusion | flops 6042746880 | bytes 12320768 | tf_op jit(solution)/shard_map/dot_general | solution.py:12
  110.7 4.6 %all-to-all-start.1 = ((bf16[16,72,2560]{2,1,0:T(8,128)(2,1)}), bf16[16,72,2560]{2,1,0:T(8,128)(2,1)}, u32[]{:S(2)}, u32[]{:S(2)}) async-start(bf16[16,72,2560]{2,1,0:T(8,128)(2,1)} %bitcast.163), calls=%async_computation.1 | async-start | bytes 11796480 | tf_op jit(solution)/shard_map/all_to_all | solution.py:109
  118.2 2.7 collective-permute-start.5
  120.9 2.1 constant_dynamic-update-slice_fusion.6
  125.5 2.2 constant_dynamic-update-slice_fusion.3
  127.7 3.4 collective-permute-done.4
  131.0 2.0 constant_dynamic-update-slice_fusion.2
  133.1 13.7 %collective-permute-done.5 = bf16[144,2560]{1,0:T(8,128)(2,1)S(1)} collective-permute-done((bf16[144,2560]{1,0:T(8,128)(2,1)}, bf16[144,2560]{1,0:T(8,128)(2,1)S(1)}, u32[]{:S(2)}, u32[]{:S(2)}) %collective-permute-start.5) | collective-permute-done | bytes 737312 | tf_op jit(solution)/shard_map/ppermute | solution.py:41
  147.7 14.9 %collective-permute-done.6 = bf16[144,2560]{1,0:T(8,128)(2,1)S(1)} collective-permute-done((bf16[144,2560]{1,0:T(8,128)(2,1)}, bf16[144,2560]{1,0:T(8,128)(2,1)S(1)}, u32[]{:S(2)}, u32[]{:S(2)}) %collective-permute-start.6) | collective-permute-done | bytes 737312 | tf_op jit(solution)/shard_map/ppermute | solution.py:41
  163.5 9.9 %fusion.4 = f32[1152,768]{0,1:T(8,128)} fusion(bf16[1152,2560]{1,0:T(8,128)(2,1)} %constant_dynamic-update-slice_fusion, bf16[1,2560,768]{2,1,0:T(8,128)(2,1)S(1)} %copy-done.35), kind=kOutput, calls=%fused_computation.18 | convolution fusion | flops 4529848320 | bytes 13369344 | tf_op jit(solution)/shard_map/dot_general | solution.py:12
  173.4 7.2 %fusion.7 = f32[1152,768]{0,1:T(8,128)} fusion(bf16[1152,2560]{1,0:T(8,128)(2,1)S(1)} %copy-done.34, bf16[1,2560,768]{2,1,0:T(8,128)(2,1)S(1)} %copy-done.36), kind=kOutput, calls=%fused_computation.21 | convolution fusion | flops 4529848320 | bytes 13369344 | tf_op jit(solution)/shard_map/dot_general | solution.py:12
  180.6 24.9 %all-to-all-done.1 = bf16[16,72,2560]{2,1,0:T(8,128)(2,1)} async-done(((bf16[16,72,2560]{2,1,0:T(8,128)(2,1)}), bf16[16,72,2560]{2,1,0:T(8,128)(2,1)}, u32[]{:S(2)}, u32[]{:S(2)}) %all-to-all-start.1) | async-done | bytes 5898272 | tf_op jit(solution)/shard_map/all_to_all | solution.py:109
  205.4 21.0 %multiply_reduce_fusion = (bf16[1152]{0:T(1024)(128)(2,1)S(1)}, f32[1152,768]{0,1:T(8,128)}) fusion(f32[1152,768]{0,1:T(8,128)} %fusion.7, f32[1152,768]{0,1:T(8,128)} %fusion.4, bf16[1,768,2560]{2,1,0:T(8,128)(2,1)} %param.13, bf16[1152,2560]{1,0:T(8,128)(2,1)} %bitcast.11, s32[1152]{0:T(1024)S(1)} %copy-done.19), kind=kOutput, calls=%fused_computation.34 | convolution fusion | flops 11336858624 | bytes 20454144 | tf_op jit(solution)/shard_map/dot_general | solution.py:20
  226.5 15.6 %fusion.2 = f32[1152,2560]{1,0:T(8,128)} fusion(bf16[1,2560,768]{2,1,0:T(8,128)(2,1)} %param.11, f32[1152,768]{0,1:T(8,128)} %fusion.4, f32[1152,768]{0,1:T(8,128)} %get-tuple-element.50, f32[1152,768]{0,1:T(8,128)} %fusion.7), kind=kOutput, calls=%fused_computation.16 | convolution fusion | flops 4538695680 | bytes 26345472 | tf_op jit(solution)/shard_map/dot_general | solution.py:20
  242.0 15.0 %fusion = bf16[1152,2560]{1,0:T(8,128)(2,1)} fusion(f32[1152,2560]{1,0:T(8,128)} %fusion.2, bf16[1,2560,768]{2,1,0:T(8,128)(2,1)} %param.12, f32[1152,768]{0,1:T(8,128)} %get-tuple-element.50, f32[1152,768]{0,1:T(8,128)} %fusion.4), kind=kOutput, calls=%fused_computation.1 | convolution fusion | flops 4541054976 | bytes 28704768 | tf_op jit(solution)/shard_map/dot_general | solution.py:20
  257.1 2.0 slice.122
  260.6 1.6 collective-permute-start.8
  263.1 3.2 collective-permute-start.10
  266.6 2.2 collective-permute-start.12
  268.8 2.3 collective-permute-done.8
  271.1 5.7 %collective-permute-start.13 = (bf16[144,1408]{1,0:T(8,128)(2,1)S(1)}, bf16[144,1408]{1,0:T(8,128)(2,1)S(1)}, u32[]{:S(2)}, u32[]{:S(2)}) collective-permute-start(bf16[144,1408]{1,0:T(8,128)(2,1)S(1)} %get-tuple-element.18), channel_id=1, source_target_pairs={{0,7},{1,6},{2,5},{3,4},{4,3},{5,2},{6,1},{7,0},{8,15},{9,14},{10,... | collective-permute-start | bytes 1216520 | tf_op jit(solution)/shard_map/ppermute | solution.py:41
  276.9 5.0 %collective-permute-done.9 = bf16[144,1408]{1,0:T(8,128)(2,1)S(1)} collective-permute-done((bf16[144,1408]{1,0:T(8,128)(2,1)S(1)}, bf16[144,1408]{1,0:T(8,128)(2,1)S(1)}, u32[]{:S(2)}, u32[]{:S(2)}) %collective-permute-start.9) | collective-permute-done | bytes 405536 | tf_op jit(solution)/shard_map/ppermute | solution.py:41
  281.9 9.1 %collective-permute-done.10 = bf16[144,1408]{1,0:T(8,128)(2,1)S(1)} collective-permute-done((bf16[144,1408]{1,0:T(8,128)(2,1)S(1)}, bf16[144,1408]{1,0:T(8,128)(2,1)S(1)}, u32[]{:S(2)}, u32[]{:S(2)}) %collective-permute-start.10) | collective-permute-done | bytes 405536 | tf_op jit(solution)/shard_map/ppermute | solution.py:41
  291.1 9.6 %collective-permute-done.11 = bf16[144,1408]{1,0:T(8,128)(2,1)S(1)} collective-permute-done((bf16[144,1408]{1,0:T(8,128)(2,1)S(1)}, bf16[144,1408]{1,0:T(8,128)(2,1)S(1)}, u32[]{:S(2)}, u32[]{:S(2)}) %collective-permute-start.11) | collective-permute-done | bytes 405536 | tf_op jit(solution)/shard_map/ppermute | solution.py:41
  300.8 4.2 collective-permute-done.13
  305.0 3.0 fusion.17
  307.9 3.0 fusion.14
  312.7 3.7 all-to-all-start.2
  316.4 8.0 %convolution_convert_fusion.2 = bf16[1152,1280]{1,0:T(8,128)(2,1)} fusion(bf16[1152,2560]{1,0:T(8,128)(2,1)} %fusion, s32[1152]{0:T(1024)S(1)} %copy-done.19), kind=kOutput, calls=%fused_computation.11 | convolution fusion | flops 3400187904 | bytes 5902848 | tf_op jit(solution)/shard_map/dot_general | solution.py:16
  324.4 11.0 %all-to-all-done.2 = bf16[16,24,1408]{2,1,0:T(8,128)(2,1)S(1)} async-done(((bf16[16,24,1408]{2,1,0:T(8,128)(2,1)}), bf16[16,24,1408]{2,1,0:T(8,128)(2,1)S(1)}, u32[]{:S(2)}, u32[]{:S(2)}) %all-to-all-start.2) | async-done | bytes 1081376 | tf_op jit(solution)/shard_map/all_to_all | solution.py:141
  336.4 3.7 all-to-all-start.3
  341.9 1.7 convolution_bitcast_fusion.16
  343.6 40.0 %all-to-all-done.3 = bf16[16,72,1280]{2,1,0:T(8,128)(2,1)S(1)} async-done(((bf16[16,72,1280]{2,1,0:T(8,128)(2,1)}), bf16[16,72,1280]{2,1,0:T(8,128)(2,1)S(1)}, u32[]{:S(2)}, u32[]{:S(2)}) %all-to-all-start.3) | async-done | bytes 2949152 | tf_op jit(solution)/shard_map/all_to_all | solution.py:145
  385.0 1.9 collective-permute-start.14
  389.5 1.9 collective-permute-start.16
  392.7 2.9 collective-permute-start.17
  400.1 2.3 collective-permute-start.19
  405.4 8.2 %collective-permute-done.17 = bf16[128,1280]{1,0:T(8,128)(2,1)S(1)} collective-permute-done((bf16[128,1280]{1,0:T(8,128)(2,1)S(1)}, bf16[128,1280]{1,0:T(8,128)(2,1)S(1)}, u32[]{:S(2)}, u32[]{:S(2)}) %collective-permute-start.17) | collective-permute-done | bytes 327712 | tf_op jit(solution)/shard_map/ppermute | solution.py:41
  413.6 7.2 %collective-permute-done.18 = bf16[128,1280]{1,0:T(8,128)(2,1)S(1)} collective-permute-done((bf16[128,1280]{1,0:T(8,128)(2,1)S(1)}, bf16[128,1280]{1,0:T(8,128)(2,1)S(1)}, u32[]{:S(2)}, u32[]{:S(2)}) %collective-permute-start.18) | collective-permute-done | bytes 327712 | tf_op jit(solution)/shard_map/ppermute | solution.py:41
  420.8 4.0 collective-permute-done.19
  424.8 7.1 %collective-permute-done.20 = bf16[128,1280]{1,0:T(8,128)(2,1)S(1)} collective-permute-done((bf16[128,1280]{1,0:T(8,128)(2,1)S(1)}, bf16[128,1280]{1,0:T(8,128)(2,1)S(1)}, u32[]{:S(2)}, u32[]{:S(2)}) %collective-permute-start.20) | collective-permute-done | bytes 327712 | tf_op jit(solution)/shard_map/ppermute | solution.py:41
  (191 shorter events, 51.8 us)
Async XLA Ops:
  7.2 90.3 %all-gather.2.cloned.1.call-start = ((), (), s32[]{:S(2)}) async-start(), calls=%async_computation.4 | async-start | bytes 6193152 | tf_op jit(solution)/shard_map/all_gather | solution.py:66
  12.7 0.6 copy-start.5
  15.4 38.5 %all-to-all-start = ((bf16[16,24,2688]{2,1,0:T(8,128)(2,1)}), bf16[16,24,2688]{2,1,0:T(8,128)(2,1)S(1)}, u32[]{:S(2)}, u32[]{:S(2)}) async-start(bf16[16,24,2688]{2,1,0:T(8,128)(2,1)} %bitcast.2), calls=%async_computation | async-start | bytes 4128768 | tf_op jit(solution)/shard_map/all_to_all | solution.py:74
  24.6 35.6 %copy-start.24 = (f32[8]{0:T(128)}, f32[8]{0:T(128)S(1)}, u32[]{:S(2)}) copy-start(f32[8]{0:T(128)S(1)} %add_convert_fusion.2) | copy-start | bytes 100
  25.7 34.4 %copy-start.25 = (pred[8]{0:T(512)(128)(4,1)}, pred[8]{0:T(512)(128)(4,1)S(1)}, u32[]{:S(2)}) copy-start(pred[8]{0:T(512)(128)(4,1)S(1)} %get-tuple-element.57) | copy-start | bytes 28
  25.7 34.4 %copy-start.26 = (pred[8]{0:T(512)(128)(4,1)}, pred[8]{0:T(512)(128)(4,1)S(1)}, u32[]{:S(2)}) copy-start(pred[8]{0:T(512)(128)(4,1)S(1)} %get-tuple-element.58) | copy-start | bytes 28
  25.8 34.4 %copy-start.27 = (pred[8]{0:T(512)(128)(4,1)}, pred[8]{0:T(512)(128)(4,1)S(1)}, u32[]{:S(2)}) copy-start(pred[8]{0:T(512)(128)(4,1)S(1)} %get-tuple-element.51) | copy-start | bytes 28
  25.8 34.4 %copy-start.28 = (pred[8]{0:T(512)(128)(4,1)}, pred[8]{0:T(512)(128)(4,1)S(1)}, u32[]{:S(2)}) copy-start(pred[8]{0:T(512)(128)(4,1)S(1)} %get-tuple-element.52) | copy-start | bytes 28
  25.8 34.4 %copy-start.29 = (pred[8]{0:T(512)(128)(4,1)}, pred[8]{0:T(512)(128)(4,1)S(1)}, u32[]{:S(2)}) copy-start(pred[8]{0:T(512)(128)(4,1)S(1)} %get-tuple-element.53) | copy-start | bytes 28
  25.8 34.4 %copy-start.30 = (pred[8]{0:T(512)(128)(4,1)}, pred[8]{0:T(512)(128)(4,1)S(1)}, u32[]{:S(2)}) copy-start(pred[8]{0:T(512)(128)(4,1)S(1)} %get-tuple-element.54) | copy-start | bytes 28
  25.8 34.4 %copy-start.31 = (pred[8]{0:T(512)(128)(4,1)}, pred[8]{0:T(512)(128)(4,1)S(1)}, u32[]{:S(2)}) copy-start(pred[8]{0:T(512)(128)(4,1)S(1)} %get-tuple-element.55) | copy-start | bytes 28
  25.9 34.4 %copy-start.32 = (pred[8]{0:T(512)(128)(4,1)}, pred[8]{0:T(512)(128)(4,1)S(1)}, u32[]{:S(2)}) copy-start(pred[8]{0:T(512)(128)(4,1)S(1)} %get-tuple-element.56) | copy-start | bytes 28
  56.5 3.7 copy-start.14
  57.9 60.2 %collective-permute-start = (bf16[144,2560]{1,0:T(8,128)(2,1)}, bf16[144,2560]{1,0:T(8,128)(2,1)}, u32[]{:S(2)}, u32[]{:S(2)}) collective-permute-start(bf16[144,2560]{1,0:T(8,128)(2,1)} %convolution_convert_fusion.10), channel_id=1, source_target_pairs={{0,1},{1,0},{2,3},{3,2},{4,5},{5,4},{6,7},{7,6},{8,9},{9,8},{10,11... | collective-permute-start | bytes 2211848 | tf_op jit(solution)/shard_map/ppermute | solution.py:41
  60.2 0.6 copy-start.15
  62.3 60.7 %collective-permute-start.1 = (bf16[144,2560]{1,0:T(8,128)(2,1)}, bf16[144,2560]{1,0:T(8,128)(2,1)S(1)}, u32[]{:S(2)}, u32[]{:S(2)}) collective-permute-start(bf16[144,2560]{1,0:T(8,128)(2,1)} %convolution_convert_fusion.9), channel_id=1, source_target_pairs={{0,2},{1,3},{2,0},{3,1},{4,6},{5,7},{6,4},{7,5},{8,10},{9,11},{10,... | collective-permute-start | bytes 2211848 | tf_op jit(solution)/shard_map/ppermute | solution.py:41
  63.7 0.6 copy-start.9
  65.7 58.9 %collective-permute-start.2 = (bf16[144,2560]{1,0:T(8,128)(2,1)}, bf16[144,2560]{1,0:T(8,128)(2,1)S(1)}, u32[]{:S(2)}, u32[]{:S(2)}) collective-permute-start(bf16[144,2560]{1,0:T(8,128)(2,1)} %convolution_convert_fusion.8), channel_id=1, source_target_pairs={{0,3},{1,2},{2,1},{3,0},{4,7},{5,6},{6,5},{7,4},{8,11},{9,10},{10,... | collective-permute-start | bytes 2211848 | tf_op jit(solution)/shard_map/ppermute | solution.py:41
  66.8 9.9 %copy-start.11 = (f32[384]{0:T(512)}, f32[384]{0:T(512)S(1)}, u32[]{:S(2)}) copy-start(f32[384]{0:T(512)S(1)} %eq.496) | copy-start | bytes 4612
  68.3 57.2 %collective-permute-start.3 = (bf16[144,2560]{1,0:T(8,128)(2,1)}, bf16[144,2560]{1,0:T(8,128)(2,1)}, u32[]{:S(2)}, u32[]{:S(2)}) collective-permute-start(bf16[144,2560]{1,0:T(8,128)(2,1)} %convolution_convert_fusion.7), channel_id=1, source_target_pairs={{0,4},{1,5},{2,6},{3,7},{4,0},{5,1},{6,2},{7,3},{8,12},{9,13},{10,... | collective-permute-start | bytes 2211848 | tf_op jit(solution)/shard_map/ppermute | solution.py:41
  74.7 56.4 %collective-permute-start.4 = (bf16[144,2560]{1,0:T(8,128)(2,1)}, bf16[144,2560]{1,0:T(8,128)(2,1)}, u32[]{:S(2)}, u32[]{:S(2)}) collective-permute-start(bf16[144,2560]{1,0:T(8,128)(2,1)} %convolution_convert_fusion.6), channel_id=1, source_target_pairs={{0,5},{1,4},{2,7},{3,6},{4,1},{5,0},{6,3},{7,2},{8,13},{9,12},{10,... | collective-permute-start | bytes 2211848 | tf_op jit(solution)/shard_map/ppermute | solution.py:41
  77.5 17.1 %copy-start.7 = (f32[384]{0:T(512)S(1)}, f32[384]{0:T(512)}, u32[]{:S(2)}) copy-start(f32[384]{0:T(512)} %eq.508) | copy-start | bytes 4612
  82.6 8.5 %copy-start.20 = (pred[1152,384]{1,0:T(8,128)(4,1)}, pred[1152,384]{1,0:T(8,128)(4,1)S(1)}, u32[]{:S(2)}) copy-start(pred[1152,384]{1,0:T(8,128)(4,1)S(1)} %fusion.144) | copy-start | bytes 1327108
  96.0 3.4 copy-start.17
  96.0 3.4 copy-start.4
  97.4 1.7 copy-start.22
  99.1 11.6 %copy-start.3 = (f32[1024,6]{0,1:T(8,128)}, f32[1024,6]{0,1:T(8,128)S(1)}, u32[]{:S(2)}) copy-start(f32[1024,6]{0,1:T(8,128)S(1)} %copy.41) | copy-start | bytes 73732
  99.4 11.3 %copy-start.1 = (f32[1024,16]{0,1:T(8,128)}, f32[1024,16]{0,1:T(8,128)S(1)}, u32[]{:S(2)}) copy-start(f32[1024,16]{0,1:T(8,128)S(1)} %fusion.157) | copy-start | bytes 196612
  110.7 4.7 %copy-start.10 = (f32[384]{0:T(512)S(1)}, f32[384]{0:T(512)}, u32[]{:S(2)}) copy-start(f32[384]{0:T(512)} %copy-done.9) | copy-start | bytes 4612
  110.7 5.4 %copy-start.18 = (f32[384]{0:T(512)S(1)}, f32[384]{0:T(512)}, u32[]{:S(2)}) copy-start(f32[384]{0:T(512)} %get-tuple-element.10) | copy-start | bytes 4612
  110.7 6.1 %copy-start.12 = (f32[384]{0:T(512)S(1)}, f32[384]{0:T(512)}, u32[]{:S(2)}) copy-start(f32[384]{0:T(512)} %copy-done.11) | copy-start | bytes 4612
  110.7 6.7 %copy-start.13 = (f32[384]{0:T(512)S(1)}, f32[384]{0:T(512)}, u32[]{:S(2)}) copy-start(f32[384]{0:T(512)} %eq.502) | copy-start | bytes 4612
  110.7 94.7 %all-to-all-start.1 = ((bf16[16,72,2560]{2,1,0:T(8,128)(2,1)}), bf16[16,72,2560]{2,1,0:T(8,128)(2,1)}, u32[]{:S(2)}, u32[]{:S(2)}) async-start(bf16[16,72,2560]{2,1,0:T(8,128)(2,1)} %bitcast.163), calls=%async_computation.1 | async-start | bytes 11796480 | tf_op jit(solution)/shard_map/all_to_all | solution.py:109
  118.2 28.6 %collective-permute-start.5 = (bf16[144,2560]{1,0:T(8,128)(2,1)}, bf16[144,2560]{1,0:T(8,128)(2,1)S(1)}, u32[]{:S(2)}, u32[]{:S(2)}) collective-permute-start(bf16[144,2560]{1,0:T(8,128)(2,1)} %convolution_convert_fusion.5), channel_id=1, source_target_pairs={{0,6},{1,7},{2,4},{3,5},{4,2},{5,3},{6,0},{7,1},{8,14},{9,15},{10,... | collective-permute-start | bytes 2211848 | tf_op jit(solution)/shard_map/ppermute | solution.py:41
  123.0 39.6 %collective-permute-start.6 = (bf16[144,2560]{1,0:T(8,128)(2,1)}, bf16[144,2560]{1,0:T(8,128)(2,1)S(1)}, u32[]{:S(2)}, u32[]{:S(2)}) collective-permute-start(bf16[144,2560]{1,0:T(8,128)(2,1)} %convolution_convert_fusion.4), channel_id=1, source_target_pairs={{0,7},{1,6},{2,5},{3,4},{4,3},{5,2},{6,1},{7,0},{8,15},{9,14},{10,... | collective-permute-start | bytes 2211848 | tf_op jit(solution)/shard_map/ppermute | solution.py:41
  125.5 38.0 %copy-start.35 = (bf16[1,2560,768]{2,1,0:T(8,128)(2,1)S(1)}, bf16[1,2560,768]{2,1,0:T(8,128)(2,1)}, u32[]{:S(2)}) copy-start(bf16[1,2560,768]{2,1,0:T(8,128)(2,1)} %param.11) | copy-start | bytes 11796484
  163.5 9.9 %copy-start.34 = (bf16[1152,2560]{1,0:T(8,128)(2,1)S(1)}, bf16[1152,2560]{1,0:T(8,128)(2,1)}, u32[]{:S(2)}) copy-start(bf16[1152,2560]{1,0:T(8,128)(2,1)} %constant_dynamic-update-slice_fusion) | copy-start | bytes 17694724
  163.5 9.9 %copy-start.36 = (bf16[1,2560,768]{2,1,0:T(8,128)(2,1)S(1)}, bf16[1,2560,768]{2,1,0:T(8,128)(2,1)}, u32[]{:S(2)}) copy-start(bf16[1,2560,768]{2,1,0:T(8,128)(2,1)} %param.12) | copy-start | bytes 11796484
  173.4 32.0 %copy-start.19 = (s32[1152]{0:T(1024)S(1)}, s32[1152]{0:T(1024)}, u32[]{:S(2)}) copy-start(s32[1152]{0:T(1024)} %fusion.177) | copy-start | bytes 13828
  257.1 2.0 copy-start.33
  259.3 1.2 copy-start.8
  259.4 1.2 copy-start.21
  259.6 6.9 %collective-permute-start.7 = (bf16[144,1408]{1,0:T(8,128)(2,1)S(1)}, bf16[144,1408]{1,0:T(8,128)(2,1)S(1)}, u32[]{:S(2)}, u32[]{:S(2)}) collective-permute-start(bf16[144,1408]{1,0:T(8,128)(2,1)S(1)} %get-tuple-element.20), channel_id=1, source_target_pairs={{0,1},{1,0},{2,3},{3,2},{4,5},{5,4},{6,7},{7,6},{8,9},{9,8},{10,11... | collective-permute-start | bytes 1216520 | tf_op jit(solution)/shard_map/ppermute | solution.py:41
  260.6 10.5 %collective-permute-start.8 = (bf16[144,1408]{1,0:T(8,128)(2,1)S(1)}, bf16[144,1408]{1,0:T(8,128)(2,1)S(1)}, u32[]{:S(2)}, u32[]{:S(2)}) collective-permute-start(bf16[144,1408]{1,0:T(8,128)(2,1)S(1)} %get-tuple-element.21), channel_id=1, source_target_pairs={{0,2},{1,3},{2,0},{3,1},{4,6},{5,7},{6,4},{7,5},{8,10},{9,11},{10,... | collective-permute-start | bytes 1216520 | tf_op jit(solution)/shard_map/ppermute | solution.py:41
  262.3 19.6 %collective-permute-start.9 = (bf16[144,1408]{1,0:T(8,128)(2,1)S(1)}, bf16[144,1408]{1,0:T(8,128)(2,1)S(1)}, u32[]{:S(2)}, u32[]{:S(2)}) collective-permute-start(bf16[144,1408]{1,0:T(8,128)(2,1)S(1)} %get-tuple-element.22), channel_id=1, source_target_pairs={{0,3},{1,2},{2,1},{3,0},{4,7},{5,6},{6,5},{7,4},{8,11},{9,10},{10,... | collective-permute-start | bytes 1216520 | tf_op jit(solution)/shard_map/ppermute | solution.py:41
  263.1 27.9 %collective-permute-start.10 = (bf16[144,1408]{1,0:T(8,128)(2,1)S(1)}, bf16[144,1408]{1,0:T(8,128)(2,1)S(1)}, u32[]{:S(2)}, u32[]{:S(2)}) collective-permute-start(bf16[144,1408]{1,0:T(8,128)(2,1)S(1)} %get-tuple-element.23), channel_id=1, source_target_pairs={{0,4},{1,5},{2,6},{3,7},{4,0},{5,1},{6,2},{7,3},{8,12},{9,13},{10,... | collective-permute-start | bytes 1216520 | tf_op jit(solution)/shard_map/ppermute | solution.py:41
  266.3 34.4 %collective-permute-start.11 = (bf16[144,1408]{1,0:T(8,128)(2,1)S(1)}, bf16[144,1408]{1,0:T(8,128)(2,1)S(1)}, u32[]{:S(2)}, u32[]{:S(2)}) collective-permute-start(bf16[144,1408]{1,0:T(8,128)(2,1)S(1)} %get-tuple-element.24), channel_id=1, source_target_pairs={{0,5},{1,4},{2,7},{3,6},{4,1},{5,0},{6,3},{7,2},{8,13},{9,12},{10,... | collective-permute-start | bytes 1216520 | tf_op jit(solution)/shard_map/ppermute | solution.py:41
  266.6 34.1 %collective-permute-start.12 = (bf16[144,1408]{1,0:T(8,128)(2,1)S(1)}, bf16[144,1408]{1,0:T(8,128)(2,1)S(1)}, u32[]{:S(2)}, u32[]{:S(2)}) collective-permute-start(bf16[144,1408]{1,0:T(8,128)(2,1)S(1)} %get-tuple-element.25), channel_id=1, source_target_pairs={{0,6},{1,7},{2,4},{3,5},{4,2},{5,3},{6,0},{7,1},{8,14},{9,15},{10,... | collective-permute-start | bytes 1216520 | tf_op jit(solution)/shard_map/ppermute | solution.py:41
  271.1 33.8 %collective-permute-start.13 = (bf16[144,1408]{1,0:T(8,128)(2,1)S(1)}, bf16[144,1408]{1,0:T(8,128)(2,1)S(1)}, u32[]{:S(2)}, u32[]{:S(2)}) collective-permute-start(bf16[144,1408]{1,0:T(8,128)(2,1)S(1)} %get-tuple-element.18), channel_id=1, source_target_pairs={{0,7},{1,6},{2,5},{3,4},{4,3},{5,2},{6,1},{7,0},{8,15},{9,14},{10,... | collective-permute-start | bytes 1216520 | tf_op jit(solution)/shard_map/ppermute | solution.py:41
  312.7 22.7 %all-to-all-start.2 = ((bf16[16,24,1408]{2,1,0:T(8,128)(2,1)}), bf16[16,24,1408]{2,1,0:T(8,128)(2,1)S(1)}, u32[]{:S(2)}, u32[]{:S(2)}) async-start(bf16[16,24,1408]{2,1,0:T(8,128)(2,1)} %pad_maximum_fusion), calls=%async_computation.2 | async-start | bytes 2162688 | tf_op jit(solution)/shard_map/all_to_all | solution.py:141
  335.4 1.0 copy-start
  335.4 5.6 %copy-start.23 = (f32[16]{0:T(128)S(1)}, f32[16]{0:T(128)}, u32[]{:S(2)}) copy-start(f32[16]{0:T(128)} %add_convert_fusion.1) | copy-start | bytes 196
  335.4 6.5 %copy-start.2 = (f32[1024,16]{0,1:T(8,128)S(1)}, f32[1024,16]{0,1:T(8,128)}, u32[]{:S(2)}) copy-start(f32[1024,16]{0,1:T(8,128)} %copy-done.1) | copy-start | bytes 196612
  335.4 6.5 %copy-start.6 = (f32[16,128]{1,0:T(8,128)S(1)}, f32[16,128]{1,0:T(8,128)}, u32[]{:S(2)}) copy-start(f32[16,128]{1,0:T(8,128)} %copy-done.5) | copy-start | bytes 24580
  336.4 47.3 %all-to-all-start.3 = ((bf16[16,72,1280]{2,1,0:T(8,128)(2,1)}), bf16[16,72,1280]{2,1,0:T(8,128)(2,1)S(1)}, u32[]{:S(2)}, u32[]{:S(2)}) async-start(bf16[16,72,1280]{2,1,0:T(8,128)(2,1)} %bitcast.164), calls=%async_computation.3 | async-start | bytes 5898240 | tf_op jit(solution)/shard_map/all_to_all | solution.py:145
  385.0 15.1 %collective-permute-start.14 = (bf16[128,1280]{1,0:T(8,128)(2,1)S(1)}, bf16[128,1280]{1,0:T(8,128)(2,1)S(1)}, u32[]{:S(2)}, u32[]{:S(2)}) collective-permute-start(bf16[128,1280]{1,0:T(8,128)(2,1)S(1)} %fusion.29), channel_id=1, source_target_pairs={{0,1},{1,0},{2,3},{3,2},{4,5},{5,4},{6,7},{7,6},{8,9},{9,8},{10,11... | collective-permute-start | bytes 983048 | tf_op jit(solution)/shard_map/ppermute | solution.py:41
  388.1 14.3 %collective-permute-start.15 = (bf16[128,1280]{1,0:T(8,128)(2,1)S(1)}, bf16[128,1280]{1,0:T(8,128)(2,1)S(1)}, u32[]{:S(2)}, u32[]{:S(2)}) collective-permute-start(bf16[128,1280]{1,0:T(8,128)(2,1)S(1)} %fusion.30), channel_id=1, source_target_pairs={{0,2},{1,3},{2,0},{3,1},{4,6},{5,7},{6,4},{7,5},{8,10},{9,11},{10,... | collective-permute-start | bytes 983048 | tf_op jit(solution)/shard_map/ppermute | solution.py:41
  389.5 15.8 %collective-permute-start.16 = (bf16[128,1280]{1,0:T(8,128)(2,1)S(1)}, bf16[128,1280]{1,0:T(8,128)(2,1)S(1)}, u32[]{:S(2)}, u32[]{:S(2)}) collective-permute-start(bf16[128,1280]{1,0:T(8,128)(2,1)S(1)} %fusion.31), channel_id=1, source_target_pairs={{0,3},{1,2},{2,1},{3,0},{4,7},{5,6},{6,5},{7,4},{8,11},{9,10},{10,... | collective-permute-start | bytes 983048 | tf_op jit(solution)/shard_map/ppermute | solution.py:41
  392.7 20.9 %collective-permute-start.17 = (bf16[128,1280]{1,0:T(8,128)(2,1)S(1)}, bf16[128,1280]{1,0:T(8,128)(2,1)S(1)}, u32[]{:S(2)}, u32[]{:S(2)}) collective-permute-start(bf16[128,1280]{1,0:T(8,128)(2,1)S(1)} %fusion.32), channel_id=1, source_target_pairs={{0,4},{1,5},{2,6},{3,7},{4,0},{5,1},{6,2},{7,3},{8,12},{9,13},{10,... | collective-permute-start | bytes 983048 | tf_op jit(solution)/shard_map/ppermute | solution.py:41
  396.9 23.9 %collective-permute-start.18 = (bf16[128,1280]{1,0:T(8,128)(2,1)S(1)}, bf16[128,1280]{1,0:T(8,128)(2,1)S(1)}, u32[]{:S(2)}, u32[]{:S(2)}) collective-permute-start(bf16[128,1280]{1,0:T(8,128)(2,1)S(1)} %fusion.33), channel_id=1, source_target_pairs={{0,5},{1,4},{2,7},{3,6},{4,1},{5,0},{6,3},{7,2},{8,13},{9,12},{10,... | collective-permute-start | bytes 983048 | tf_op jit(solution)/shard_map/ppermute | solution.py:41
  398.8 4.3 copy-start.16
  400.1 24.7 %collective-permute-start.19 = (bf16[128,1280]{1,0:T(8,128)(2,1)S(1)}, bf16[128,1280]{1,0:T(8,128)(2,1)S(1)}, u32[]{:S(2)}, u32[]{:S(2)}) collective-permute-start(bf16[128,1280]{1,0:T(8,128)(2,1)S(1)} %fusion.34), channel_id=1, source_target_pairs={{0,6},{1,7},{2,4},{3,5},{4,2},{5,3},{6,0},{7,1},{8,14},{9,15},{10,... | collective-permute-start | bytes 983048 | tf_op jit(solution)/shard_map/ppermute | solution.py:41
  402.4 29.5 %collective-permute-start.20 = (bf16[128,1280]{1,0:T(8,128)(2,1)S(1)}, bf16[128,1280]{1,0:T(8,128)(2,1)S(1)}, u32[]{:S(2)}, u32[]{:S(2)}) collective-permute-start(bf16[128,1280]{1,0:T(8,128)(2,1)S(1)} %fusion.35), channel_id=1, source_target_pairs={{0,7},{1,6},{2,5},{3,4},{4,3},{5,2},{6,1},{7,0},{8,15},{9,14},{10,... | collective-permute-start | bytes 983048 | tf_op jit(solution)/shard_map/ppermute | solution.py:41
Sparse Core Ops, SparseCore 0:
  11.3 41.2 all-gather.1
